TPU v7x, 32 devices: a whole 2x2x4 slice. The times are simulated.
32 devices in a mesh: section: 2 (over core), blk: 8 (over z, y), head: 2 (over x).
Axes of the slice: x: 2, y: 2, z: 4, core: 2. Of those that a mesh axis runs over, the one named last changes fastest.
Arguments:
- queries: bfloat16 [2, 2048, 8192], P('section', ('blk', 'head')), may hold values from -96 to 96
- key_vectors: bfloat16 [2, 2048, 1024], P('section', ('blk', 'head')), may hold values from -6 to 6
- value_vectors: bfloat16 [2, 2048, 1024], P('section', ('blk', 'head')), may hold values from -6 to 6
- residual: bfloat16 [2048, 8192], P('blk', 'head'), may hold values from -128 to 128
- pair_order: int32 [8], replicated, may hold values from 0 to 7, as said below
- probe_gain: float32 [2, 8192], P('section', 'head'), may hold values from 0.1 to 1.9
- probe_weight: float32 [2, 8192], P('section', 'head'), may hold values from -0.0625 to 0.0625
Outputs:
- hidden_out: bfloat16 [2, 2048, 8192], P('section', 'blk', 'head')
- rewards: float32 [2, 2048], P('section', 'blk')
Inputs may be any that keep to these rules, and one draw needn't show every extreme that they name: `pair_order`: each value appears once.
All inputs are finite; a program needn't handle non-finite values.
Results may differ from a plain program's by a relative error of at most 0.004.
Values may be sent and summed in bfloat16 or wider, within the bound.
A program may use at most 64 MiB of HBM per device.

v0:
```python
import jax
import jax.numpy as jnp
from jax import lax
from jax.sharding import PartitionSpec as P

D = 8192
HEADS = 64
KV_HEADS = 8
HEAD_DIM = 128


neg_start = -1e30


def passed_along(value, axis, steps):
    count = lax.axis_size(axis)
    initial, last = (max(0, -steps), min(count, count - steps))
    return lax.ppermute(value, axis, [(source, source + steps) for source in range(initial, last)])


def block_first(pair_order, first_row, span_rows):
    count = pair_order.shape[0]
    shard = first_row // (2 * span_rows)
    second = first_row % (2 * span_rows) // span_rows
    lower = jnp.sum(jnp.where(jnp.arange(count, dtype=jnp.int32) == shard, pair_order, 0))
    which = jnp.where(second == 0, lower, 2 * count - 1 - lower)
    return which * span_rows


def update(state, q_part, q_places, key_block, value_block, key_places, factor):
    maxima, totals, accum = state
    scores = (
        jnp.einsum("tkgd,skd->tkgs", q_part, key_block, preferred_element_type=jnp.float32) * factor
    )
    seen = (key_places[None, :] <= q_places[:, None])[:, None, None, :]
    scores = jnp.where(seen, scores, -jnp.inf)
    new_max = jnp.maximum(maxima, jnp.max(scores, axis=-1))
    rescale = jnp.exp(maxima - new_max)
    weights = jnp.exp(scores - new_max[..., None])
    totals = totals * rescale + jnp.sum(weights, axis=-1)
    accum = accum * rescale[..., None] + jnp.einsum(
        "tkgs,skd->tkgd",
        weights.astype(jnp.bfloat16),
        value_block,
        preferred_element_type=jnp.float32,
    )
    return (new_max, totals, accum)


def body(queries, key_vectors, value_vectors, residual, pair_order, probe_gain, probe_weight):
    head_count = lax.axis_size("head")
    q_local, k_local, v_local = (
        lax.all_to_all(queries[0], "head", split_axis=1, concat_axis=0, tiled=True),
        lax.all_to_all(key_vectors[0], "head", split_axis=1, concat_axis=0, tiled=True),
        lax.all_to_all(value_vectors[0], "head", split_axis=1, concat_axis=0, tiled=True),
    )
    row_count = q_local.shape[0]
    span_rows = row_count // 2
    kv_local = KV_HEADS // head_count
    group = HEADS // KV_HEADS
    query_heads = q_local.reshape(row_count, kv_local, group, HEAD_DIM)
    blk_count = lax.axis_size("blk")
    blk_index = lax.axis_index("blk")
    lower = jnp.sum(jnp.where(jnp.arange(blk_count, dtype=jnp.int32) == blk_index, pair_order, 0))
    q_firsts = (lower * span_rows, (2 * blk_count - 1 - lower) * span_rows)
    factor = HEAD_DIM ** (-0.5)
    offsets = jnp.arange(span_rows, dtype=jnp.int32)

    def empty_state():
        return (
            jnp.full((span_rows, kv_local, group), neg_start, jnp.float32),
            jnp.zeros((span_rows, kv_local, group), jnp.float32),
            jnp.zeros((span_rows, kv_local, group, HEAD_DIM), jnp.float32),
        )

    initial = (empty_state(), empty_state())
    carry = initial
    key_piece = lax.all_gather(k_local, "blk", axis=0, tiled=True)
    value_piece = lax.all_gather(v_local, "blk", axis=0, tiled=True)
    blocks = key_piece.shape[0] // span_rows
    key_blocks = key_piece.reshape(blocks, span_rows, kv_local, HEAD_DIM)
    value_blocks = value_piece.reshape(blocks, span_rows, kv_local, HEAD_DIM)
    firsts = jnp.arange(blocks, dtype=jnp.int32) * span_rows

    def key_block(state, inputs):
        key_block_now, value_block_now, first_row = inputs
        key_base = block_first(pair_order, first_row, span_rows)
        key_places = key_base + offsets
        results = []
        for which_half in range(2):
            q_part = query_heads[which_half * span_rows : (which_half + 1) * span_rows]
            q_places = q_firsts[which_half] + offsets

            def compute(inner):
                return update(
                    inner, q_part, q_places, key_block_now, value_block_now, key_places, factor
                )

            def keep(inner):
                return inner

            results.append(
                lax.cond(
                    key_base <= q_firsts[which_half] + span_rows - 1,
                    compute,
                    keep,
                    state[which_half],
                )
            )
        return ((results[0], results[1]), None)

    carry, _ = lax.scan(key_block, carry, (key_blocks, value_blocks, firsts))
    pieces = [state[2] / state[1][..., None] for state in carry]
    attended = jnp.concatenate(pieces, axis=0).reshape(row_count, kv_local * group * HEAD_DIM)
    section_index = lax.axis_index("section")
    own_stream = (residual.astype(jnp.float32) + attended).astype(jnp.bfloat16)
    handed = passed_along(own_stream, "section", 1)
    later_stream = (handed.astype(jnp.float32) + attended).astype(jnp.bfloat16)
    stream = jnp.where(section_index == 0, own_stream, later_stream)
    widened = stream.astype(jnp.float32)
    squares = jnp.sum(widened * widened, axis=-1)
    products = jnp.sum(widened * probe_gain[0][None, :] * probe_weight[0][None, :], axis=-1)
    squares, products = lax.psum((squares, products), "head")
    reward = products * lax.rsqrt(squares / D + 1e-05)
    return (stream[None], reward[None])


def solution(mesh):
    return jax.shard_map(
        body,
        mesh=mesh,
        in_specs=(
            P("section", ("blk", "head"), None),
            P("section", ("blk", "head"), None),
            P("section", ("blk", "head"), None),
            P("blk", "head"),
            P(),
            P("section", "head"),
            P("section", "head"),
        ),
        out_specs=(P("section", "blk", "head"), P("section", "blk")),
        check_vma=False,
    )
```

profile of v0, /device:TPU:4, one launch (start us, length us, event | category | flops | bytes accessed | tf_op | source)
XLA Modules:
  0.0 333.9 jit_solution(12832899177722277462)
XLA Ops:
  8.3 7.8 %all_to_all.54 = bf16[128,2,512]{0,2,1:T(8,128)(2,1)S(1)} all-to-all(bf16[128,2,512]{0,2,1:T(8,128)(2,1)S(1)} %bitcast.85), channel_id=1, replica_groups=mesh['section'=2,'blk'=8,'head'=2] {'head'}, dimensions={1} | all-to-all | bytes 524288 | tf_op jit(solution)/shard_map/all_to_all | solution.py:54
  18.2 7.6 %all_to_all.55 = bf16[128,2,512]{0,2,1:T(8,128)(2,1)S(1)} all-to-all(bf16[128,2,512]{0,2,1:T(8,128)(2,1)S(1)} %bitcast.86), channel_id=1, replica_groups=mesh['section'=2,'blk'=8,'head'=2] {'head'}, dimensions={1} | all-to-all | bytes 524288 | tf_op jit(solution)/shard_map/all_to_all | solution.py:55
  26.7 3.3 all_to_all.48
  30.0 2.6 copy.29
  32.6 3.9 %all-to-all-start.2 = ((bf16[128,2,4096]{2,0,1:T(8,128)(2,1)}), bf16[128,2,4096]{2,0,1:T(8,128)(2,1)S(1)}, u32[]{:S(2)}, u32[]{:S(2)}) async-start(bf16[128,2,4096]{2,0,1:T(8,128)(2,1)} %copy.29), calls=%async_computation.2 | async-start | bytes 4194304 | tf_op jit(solution)/shard_map/all_to_all | solution.py:53
  38.5 21.0 %all-to-all-done.2 = bf16[128,2,4096]{2,0,1:T(8,128)(2,1)S(1)} async-done(((bf16[128,2,4096]{2,0,1:T(8,128)(2,1)}), bf16[128,2,4096]{2,0,1:T(8,128)(2,1)S(1)}, u32[]{:S(2)}, u32[]{:S(2)}) %all-to-all-start.2) | async-done | bytes 2097184 | tf_op jit(solution)/shard_map/all_to_all | solution.py:53
  62.1 3.8 %all-gather.3.cloned.1.call-done = bf16[2048,512]{1,0:T(8,128)(2,1)} async-done(((bf16[256,512]{1,0:T(8,128)(2,1)}), bf16[2048,512]{1,0:T(8,128)(2,1)}) %all-gather.3.cloned.1.call-update) | async-done | bytes 2097168 | tf_op jit(solution)/shard_map/all_gather | solution.py:78
  65.8 4.0 %reshape.89 = bf16[16,128,4,128]{3,2,1,0:T(4,128)(2,1)} reshape(bf16[2048,512]{1,0:T(8,128)(2,1)} %all-gather.3.cloned.1.call-done) | data formatting | bytes 4194304 | tf_op jit(solution)/shard_map/reshape | solution.py:81
  69.8 46.0 %all-gather.5.cloned.1.call-done = bf16[2048,512]{1,0:T(8,128)(2,1)} async-done(((bf16[256,512]{1,0:T(8,128)(2,1)}), bf16[2048,512]{1,0:T(8,128)(2,1)}) %all-gather.5.cloned.1.call-update) | async-done | bytes 2097168 | tf_op jit(solution)/shard_map/all_gather | solution.py:79
  115.8 4.0 %reshape.90 = bf16[16,128,4,128]{3,2,1,0:T(4,128)(2,1)} reshape(bf16[2048,512]{1,0:T(8,128)(2,1)} %all-gather.5.cloned.1.call-done) | data formatting | bytes 4194304 | tf_op jit(solution)/shard_map/reshape | solution.py:82
  121.6 177.5 %while.25 = (s32[]{:T(128)}, f32[128,4,8]{0,2,1:T(8,128)S(1)}, f32[128,4,8]{0,2,1:T(8,128)S(1)}, f32[128,4,8,128]{3,0,2,1:T(8,128)}, f32[128,4,8]{0,2,1:T(8,128)...) while((s32[]{:T(128)}, f32[128,4,8]{0,2,1:T(8,128)S(1)}, ...), condition=%wide.region_11.12_spmd.clone.clone, body=%wide.region_1.11_spmd.clone.clone.sunk | while | flops 546357696 | bytes 42014720 | solution.py:112
  128.3 5.0 %conditional.8 = ((f32[128,4,8]{0,2,1:T(8,128)S(1)}, f32[128,4,8]{0,2,1:T(8,128)S(1)}, f32[128,4,8,128]{3,0,2,1:T(8,128)})) conditional(s32[]{:T(128)} %convert_element_type.68, (f32[128,4,8]{0,2,1:T(8,128)S(1)}, f32[128,4,8]{0,2,1:T(8,128)S(1)}, f32[128,4,8,128]{3,0,2,1:T(8,128)}) %tuple.77, (s32[128]{0:T(128)S(1)}, s32[]{:T(128)}, ...), branch_computations={%region_3.3_spmd, %region_4.6_spmd} | conditional | flops 273178752 | bytes 28870748 | solution.py:103
  133.4 3.5 %conditional.9 = ((f32[128,4,8]{0,2,1:T(8,128)S(1)}, f32[128,4,8]{0,2,1:T(8,128)S(1)}, f32[128,4,8,128]{3,0,2,1:T(8,128)S(1)})) conditional(s32[]{:T(128)} %convert_element_type.69, (f32[128,4,8]{0,2,1:T(8,128)S(1)}, f32[128,4,8]{0,2,1:T(8,128)S(1)}, f32[128,4,8,128]{3,0,2,1:T(8,128)S(1)}) %tuple.79, (s32[128]{0:T(128)S(1)}, s32[]{:T(128)}, ...), branch_computations={%region_7.7_spmd, %region_8.10_spmd} | conditional | flops 273178752 | bytes 12093476 | solution.py:103
  150.4 5.0 %conditional.8 = ((f32[128,4,8]{0,2,1:T(8,128)S(1)}, f32[128,4,8]{0,2,1:T(8,128)S(1)}, f32[128,4,8,128]{3,0,2,1:T(8,128)})) conditional(s32[]{:T(128)} %convert_element_type.68, (f32[128,4,8]{0,2,1:T(8,128)S(1)}, f32[128,4,8]{0,2,1:T(8,128)S(1)}, f32[128,4,8,128]{3,0,2,1:T(8,128)}) %tuple.77, (s32[128]{0:T(128)S(1)}, s32[]{:T(128)}, ...), branch_computations={%region_3.3_spmd, %region_4.6_spmd} | conditional | flops 273178752 | bytes 28870748 | solution.py:103
  155.5 3.5 %conditional.9 = ((f32[128,4,8]{0,2,1:T(8,128)S(1)}, f32[128,4,8]{0,2,1:T(8,128)S(1)}, f32[128,4,8,128]{3,0,2,1:T(8,128)S(1)})) conditional(s32[]{:T(128)} %convert_element_type.69, (f32[128,4,8]{0,2,1:T(8,128)S(1)}, f32[128,4,8]{0,2,1:T(8,128)S(1)}, f32[128,4,8,128]{3,0,2,1:T(8,128)S(1)}) %tuple.79, (s32[128]{0:T(128)S(1)}, s32[]{:T(128)}, ...), branch_computations={%region_7.7_spmd, %region_8.10_spmd} | conditional | flops 273178752 | bytes 12093476 | solution.py:103
  165.8 3.5 %conditional.9 = ((f32[128,4,8]{0,2,1:T(8,128)S(1)}, f32[128,4,8]{0,2,1:T(8,128)S(1)}, f32[128,4,8,128]{3,0,2,1:T(8,128)S(1)})) conditional(s32[]{:T(128)} %convert_element_type.69, (f32[128,4,8]{0,2,1:T(8,128)S(1)}, f32[128,4,8]{0,2,1:T(8,128)S(1)}, f32[128,4,8,128]{3,0,2,1:T(8,128)S(1)}) %tuple.79, (s32[128]{0:T(128)S(1)}, s32[]{:T(128)}, ...), branch_computations={%region_7.7_spmd, %region_8.10_spmd} | conditional | flops 273178752 | bytes 12093476 | solution.py:103
  176.1 5.0 %conditional.8 = ((f32[128,4,8]{0,2,1:T(8,128)S(1)}, f32[128,4,8]{0,2,1:T(8,128)S(1)}, f32[128,4,8,128]{3,0,2,1:T(8,128)})) conditional(s32[]{:T(128)} %convert_element_type.68, (f32[128,4,8]{0,2,1:T(8,128)S(1)}, f32[128,4,8]{0,2,1:T(8,128)S(1)}, f32[128,4,8,128]{3,0,2,1:T(8,128)}) %tuple.77, (s32[128]{0:T(128)S(1)}, s32[]{:T(128)}, ...), branch_computations={%region_3.3_spmd, %region_4.6_spmd} | conditional | flops 273178752 | bytes 28870748 | solution.py:103
  181.1 3.5 %conditional.9 = ((f32[128,4,8]{0,2,1:T(8,128)S(1)}, f32[128,4,8]{0,2,1:T(8,128)S(1)}, f32[128,4,8,128]{3,0,2,1:T(8,128)S(1)})) conditional(s32[]{:T(128)} %convert_element_type.69, (f32[128,4,8]{0,2,1:T(8,128)S(1)}, f32[128,4,8]{0,2,1:T(8,128)S(1)}, f32[128,4,8,128]{3,0,2,1:T(8,128)S(1)}) %tuple.79, (s32[128]{0:T(128)S(1)}, s32[]{:T(128)}, ...), branch_computations={%region_7.7_spmd, %region_8.10_spmd} | conditional | flops 273178752 | bytes 12093476 | solution.py:103
  198.2 5.0 %conditional.8 = ((f32[128,4,8]{0,2,1:T(8,128)S(1)}, f32[128,4,8]{0,2,1:T(8,128)S(1)}, f32[128,4,8,128]{3,0,2,1:T(8,128)})) conditional(s32[]{:T(128)} %convert_element_type.68, (f32[128,4,8]{0,2,1:T(8,128)S(1)}, f32[128,4,8]{0,2,1:T(8,128)S(1)}, f32[128,4,8,128]{3,0,2,1:T(8,128)}) %tuple.77, (s32[128]{0:T(128)S(1)}, s32[]{:T(128)}, ...), branch_computations={%region_3.3_spmd, %region_4.6_spmd} | conditional | flops 273178752 | bytes 28870748 | solution.py:103
  203.2 3.5 %conditional.9 = ((f32[128,4,8]{0,2,1:T(8,128)S(1)}, f32[128,4,8]{0,2,1:T(8,128)S(1)}, f32[128,4,8,128]{3,0,2,1:T(8,128)S(1)})) conditional(s32[]{:T(128)} %convert_element_type.69, (f32[128,4,8]{0,2,1:T(8,128)S(1)}, f32[128,4,8]{0,2,1:T(8,128)S(1)}, f32[128,4,8,128]{3,0,2,1:T(8,128)S(1)}) %tuple.79, (s32[128]{0:T(128)S(1)}, s32[]{:T(128)}, ...), branch_computations={%region_7.7_spmd, %region_8.10_spmd} | conditional | flops 273178752 | bytes 12093476 | solution.py:103
  220.3 5.0 %conditional.8 = ((f32[128,4,8]{0,2,1:T(8,128)S(1)}, f32[128,4,8]{0,2,1:T(8,128)S(1)}, f32[128,4,8,128]{3,0,2,1:T(8,128)})) conditional(s32[]{:T(128)} %convert_element_type.68, (f32[128,4,8]{0,2,1:T(8,128)S(1)}, f32[128,4,8]{0,2,1:T(8,128)S(1)}, f32[128,4,8,128]{3,0,2,1:T(8,128)}) %tuple.77, (s32[128]{0:T(128)S(1)}, s32[]{:T(128)}, ...), branch_computations={%region_3.3_spmd, %region_4.6_spmd} | conditional | flops 273178752 | bytes 28870748 | solution.py:103
  225.3 3.5 %conditional.9 = ((f32[128,4,8]{0,2,1:T(8,128)S(1)}, f32[128,4,8]{0,2,1:T(8,128)S(1)}, f32[128,4,8,128]{3,0,2,1:T(8,128)S(1)})) conditional(s32[]{:T(128)} %convert_element_type.69, (f32[128,4,8]{0,2,1:T(8,128)S(1)}, f32[128,4,8]{0,2,1:T(8,128)S(1)}, f32[128,4,8,128]{3,0,2,1:T(8,128)S(1)}) %tuple.79, (s32[128]{0:T(128)S(1)}, s32[]{:T(128)}, ...), branch_computations={%region_7.7_spmd, %region_8.10_spmd} | conditional | flops 273178752 | bytes 12093476 | solution.py:103
  242.4 3.5 %conditional.9 = ((f32[128,4,8]{0,2,1:T(8,128)S(1)}, f32[128,4,8]{0,2,1:T(8,128)S(1)}, f32[128,4,8,128]{3,0,2,1:T(8,128)S(1)})) conditional(s32[]{:T(128)} %convert_element_type.69, (f32[128,4,8]{0,2,1:T(8,128)S(1)}, f32[128,4,8]{0,2,1:T(8,128)S(1)}, f32[128,4,8,128]{3,0,2,1:T(8,128)S(1)}) %tuple.79, (s32[128]{0:T(128)S(1)}, s32[]{:T(128)}, ...), branch_computations={%region_7.7_spmd, %region_8.10_spmd} | conditional | flops 273178752 | bytes 12093476 | solution.py:103
  252.8 3.5 %conditional.9 = ((f32[128,4,8]{0,2,1:T(8,128)S(1)}, f32[128,4,8]{0,2,1:T(8,128)S(1)}, f32[128,4,8,128]{3,0,2,1:T(8,128)S(1)})) conditional(s32[]{:T(128)} %convert_element_type.69, (f32[128,4,8]{0,2,1:T(8,128)S(1)}, f32[128,4,8]{0,2,1:T(8,128)S(1)}, f32[128,4,8,128]{3,0,2,1:T(8,128)S(1)}) %tuple.79, (s32[128]{0:T(128)S(1)}, s32[]{:T(128)}, ...), branch_computations={%region_7.7_spmd, %region_8.10_spmd} | conditional | flops 273178752 | bytes 12093476 | solution.py:103
  263.1 5.0 %conditional.8 = ((f32[128,4,8]{0,2,1:T(8,128)S(1)}, f32[128,4,8]{0,2,1:T(8,128)S(1)}, f32[128,4,8,128]{3,0,2,1:T(8,128)})) conditional(s32[]{:T(128)} %convert_element_type.68, (f32[128,4,8]{0,2,1:T(8,128)S(1)}, f32[128,4,8]{0,2,1:T(8,128)S(1)}, f32[128,4,8,128]{3,0,2,1:T(8,128)}) %tuple.77, (s32[128]{0:T(128)S(1)}, s32[]{:T(128)}, ...), branch_computations={%region_3.3_spmd, %region_4.6_spmd} | conditional | flops 273178752 | bytes 28870748 | solution.py:103
  268.1 3.5 %conditional.9 = ((f32[128,4,8]{0,2,1:T(8,128)S(1)}, f32[128,4,8]{0,2,1:T(8,128)S(1)}, f32[128,4,8,128]{3,0,2,1:T(8,128)S(1)})) conditional(s32[]{:T(128)} %convert_element_type.69, (f32[128,4,8]{0,2,1:T(8,128)S(1)}, f32[128,4,8]{0,2,1:T(8,128)S(1)}, f32[128,4,8,128]{3,0,2,1:T(8,128)S(1)}) %tuple.79, (s32[128]{0:T(128)S(1)}, s32[]{:T(128)}, ...), branch_computations={%region_7.7_spmd, %region_8.10_spmd} | conditional | flops 273178752 | bytes 12093476 | solution.py:103
  285.2 3.5 %conditional.9 = ((f32[128,4,8]{0,2,1:T(8,128)S(1)}, f32[128,4,8]{0,2,1:T(8,128)S(1)}, f32[128,4,8,128]{3,0,2,1:T(8,128)S(1)})) conditional(s32[]{:T(128)} %convert_element_type.69, (f32[128,4,8]{0,2,1:T(8,128)S(1)}, f32[128,4,8]{0,2,1:T(8,128)S(1)}, f32[128,4,8,128]{3,0,2,1:T(8,128)S(1)}) %tuple.79, (s32[128]{0:T(128)S(1)}, s32[]{:T(128)}, ...), branch_computations={%region_7.7_spmd, %region_8.10_spmd} | conditional | flops 273178752 | bytes 12093476 | solution.py:103
  295.6 3.5 %conditional.9 = ((f32[128,4,8]{0,2,1:T(8,128)S(1)}, f32[128,4,8]{0,2,1:T(8,128)S(1)}, f32[128,4,8,128]{3,0,2,1:T(8,128)S(1)})) conditional(s32[]{:T(128)} %convert_element_type.69, (f32[128,4,8]{0,2,1:T(8,128)S(1)}, f32[128,4,8]{0,2,1:T(8,128)S(1)}, f32[128,4,8,128]{3,0,2,1:T(8,128)S(1)}) %tuple.79, (s32[128]{0:T(128)S(1)}, s32[]{:T(128)}, ...), branch_computations={%region_7.7_spmd, %region_8.10_spmd} | conditional | flops 273178752 | bytes 12093476 | solution.py:103
  304.6 4.2 %fusion.20 = bf16[256,4096]{1,0:T(8,128)(2,1)S(1)} fusion(bf16[256,4096]{1,0:T(8,128)(2,1)S(1)} %copy-done.3, f32[32,8,32,128]{3,2,1,0:T(8,128)S(1)} %bitcast.72), kind=kLoop, calls=%fused_computation.41 | loop fusion | flops 3145728 | bytes 8388608 | tf_op jit(solution)/shard_map/convert_element_type | solution.py:116
  308.8 2.6 collective-permute-start
  314.0 7.6 %fusion.19 = (f32[256]{0:T(256)S(1)}, f32[256]{0:T(256)S(1)}, bf16[256,4096]{1,0:T(8,128)(2,1)}) fusion(f32[4096]{0:T(1024)S(1)} %bitcast.87, f32[4096]{0:T(1024)S(1)} %bitcast.88, bf16[256,4096]{1,0:T(8,128)(2,1)S(1)} %fusion.20, f32[32,8,32,128]{3,2,1,0:T(8,128)} %bitcast.73, bf16[256,4096]{1,0:T(8,128)(2,1)} %collective-permute-done, pred[]{:T(512)S(6)} %eq.34), kind=kLoop, calls=%fused_computation.38 | loop fusion | flops 10485248 | bytes 10520577 | tf_op jit(solution)/shard_map/reduce_sum | solution.py:121
  321.6 4.9 %all-reduce = (f32[256]{0:T(256)S(1)}, f32[256]{0:T(256)S(1)}) all-reduce(f32[256]{0:T(256)S(1)} %get-tuple-element.486, f32[256]{0:T(256)S(1)} %get-tuple-element.485), channel_id=1, replica_groups=mesh['section'=2,'blk'=8,'head'=2] {'head'}, use_global_device_ids=true, to_apply=%region_13.14 | all-reduce | flops 512 | bytes 4096 | tf_op jit(solution)/shard_map/psum | solution.py:123
  (320 shorter events, 125.7 us)
Async XLA Ops:
  7.2 58.7 %all-gather.3.cloned.1.call-start = ((), (), s32[]{:S(2)}) async-start(), calls=%async_computation.3 | async-start | bytes 2359296 | tf_op jit(solution)/shard_map/all_gather | solution.py:78
  17.0 98.7 %all-gather.5.cloned.1.call-start = ((), (), s32[]{:S(2)}) async-start(), calls=%async_computation.4 | async-start | bytes 2359296 | tf_op jit(solution)/shard_map/all_gather | solution.py:79
  32.6 3.9 %copy-start.6 = (s32[8]{0:T(128)S(1)}, s32[8]{0:T(128)}, u32[]{:S(2)}) copy-start(s32[8]{0:T(128)} %param.17) | copy-start | bytes 100
  32.6 26.8 %all-to-all-start.2 = ((bf16[128,2,4096]{2,0,1:T(8,128)(2,1)}), bf16[128,2,4096]{2,0,1:T(8,128)(2,1)S(1)}, u32[]{:S(2)}, u32[]{:S(2)}) async-start(bf16[128,2,4096]{2,0,1:T(8,128)(2,1)} %copy.29), calls=%async_computation.2 | async-start | bytes 4194304 | tf_op jit(solution)/shard_map/all_to_all | solution.py:53
  128.4 2.3 copy-start
  132.0 1.3 copy-start.1
  150.6 2.3 copy-start
  154.1 1.3 copy-start.1
  176.2 2.3 copy-start
  179.8 1.3 copy-start.1
  198.3 2.3 copy-start
  201.9 1.3 copy-start.1
  220.4 2.3 copy-start
  224.0 1.3 copy-start.1
  263.2 2.3 copy-start
  266.8 1.3 copy-start.1
  302.1 2.5 copy-start.3
  304.5 4.3 %copy-start.2 = (f32[256,4,8,128]{3,2,1,0:T(8,128)}, f32[256,4,8,128]{3,2,1,0:T(8,128)S(1)}, u32[]{:S(2)}) copy-start(f32[256,4,8,128]{3,2,1,0:T(8,128)S(1)} %copy.33) | copy-start | bytes 12582916
  304.5 9.4 %copy-start.4 = (f32[1,4096]{1,0:T(1,128)S(1)}, f32[1,4096]{1,0:T(1,128)}, u32[]{:S(2)}) copy-start(f32[1,4096]{1,0:T(1,128)} %param.19) | copy-start | bytes 49156
  304.6 9.4 %copy-start.5 = (f32[1,4096]{1,0:T(1,128)S(1)}, f32[1,4096]{1,0:T(1,128)}, u32[]{:S(2)}) copy-start(f32[1,4096]{1,0:T(1,128)} %param.18) | copy-start | bytes 49156
  308.8 5.2 %collective-permute-start = (bf16[256,4096]{1,0:T(8,128)(2,1)S(1)}, bf16[256,4096]{1,0:T(8,128)(2,1)}, u32[]{:S(2)}, u32[]{:S(2)}) collective-permute-start(bf16[256,4096]{1,0:T(8,128)(2,1)S(1)} %fusion.20), channel_id=1, source_target_pairs={{0,16},{1,17},{2,18},{3,19},{4,20},{5,21},{6,22},{7,23},{8,24},{9,... | collective-permute-start | bytes 6291464 | tf_op jit(solution)/shard_map/ppermute | solution.py:18
Sparse Core Ops, SparseCore 0:
  17.2 48.6 all-gather.2
  68.0 47.7 all-gather.4
where the time goes:
time: 340 us; the launch traced here: 334 us
  waiting for transfers between devices  73.3 us (22%)
  loops' own time  69.8 us (21%)
  local copies, waits for them, and re-layouts  61 us (18%)
  matrix products  51.8 us (15%)
  other arithmetic  35.5 us (10%)
  blocking collectives  20.3 us (6%)
  between operations  15.5 us (5%)
  starting transfers between devices  6.6 us (2%)
    another operation x1, loops' own time, body(): carry, _ = lax.scan(key_block, carry, (key_blocks, value_blocks, firsts))  68.4 us
    all_gather x1, waiting for transfers between devices, body(): value_piece = lax.all_gather(v_local, 'blk', axis=0, tiled=True)  46 us
    dot_general x17, matrix products, update(): jnp.einsum('tkgd,skd->tkgs', q_part, key_block, preferred_element_type=jn...  29.5 us
    dynamic_slice x64, local copies, waits for them, and re-layouts, body(): carry, _ = lax.scan(key_block, carry, (key_blocks, value_blocks, firsts))  28.3 us
    dot_general x17, matrix products, update(): jnp.einsum('tkgs,skd->tkgd', weights.astype(jnp.bfloat16), value_block, p...  22.4 us
    all_to_all x1, waiting for transfers between devices, body(): lax.all_to_all(queries[0], 'head', split_axis=1, concat_axis=0, tiled=True)  21 us
    reduce_sum x16, other arithmetic, block_first(): jnp.sum(jnp.where(jnp.arange(count, dtype=jnp.int32) == shard, pair_order...  11.4 us
    cond x41, local copies, waits for them, and re-layouts  7.97 us
  transfers between devices with their start and end apart: 4, of which 4 were waited for; matrix products, arithmetic and copies ran while one was open for 4% of the time, Pallas kernels for 0%

commit v1 on v0

v1 whole, which is shorter than its diff:
```python
import functools
import math

import jax
import jax.numpy as jnp
from jax import lax
from jax.experimental import pallas as pl
from jax.experimental.pallas import tpu as pltpu
from jax.sharding import PartitionSpec as P

HEAD_DIM = 128
LOW = -1e30
MESH = pl.DeviceIdType.MESH


def kernel(
    sizes,
    order_ref,
    q_ref,
    k_ref,
    v_ref,
    res_ref,
    gain_ref,
    weight_ref,
    out_ref,
    reward_ref,
    kvbufs,
    qbufs,
    base,
    accs,
    maxima,
    totals,
    squares,
    products,
    parts,
    local_sem,
    xkv_send,
    xkv_recv,
    xq_send,
    xq_recv,
    ring_send,
    ring_recv,
    hand_send,
    hand_recv,
    part_send,
    part_recv,
):
    n, heads, kvl, group, span, rows, dirs = sizes
    phases = kvl // dirs
    steps = n + 1
    width = group * HEAD_DIM
    per_half = heads // 2
    sec = lax.axis_index("section")
    me = lax.axis_index("blk")
    h = lax.axis_index("head")

    def index_of(place):
        return jnp.where(2 * place < n, 2 * place, 2 * (n - 1 - place) + 1)

    place = jnp.where(me % 2 == 0, me // 2, n - 1 - me // 2)
    right = index_of((place + 1) % n)
    left = index_of((place + n - 1) % n)

    barrier = pltpu.get_barrier_semaphore()
    for to in (left, right):
        pl.semaphore_signal(barrier, inc=1, device_id={"blk": to}, device_id_type=MESH)
    for k in range(1, heads):
        pl.semaphore_signal(barrier, inc=1, device_id={"head": (h + k) % heads}, device_id_type=MESH)
    pl.semaphore_signal(barrier, inc=1, device_id={"section": 1 - sec}, device_id_type=MESH)
    pl.semaphore_wait(barrier, heads + 2)

    def rows_of(source):
        return source // per_half, pl.ds(pl.multiple_of((source % per_half) * rows, rows), rows)

    half_own, at_own = rows_of(h)

    def local_kv(j):
        cols = pl.ds(pl.multiple_of((h * kvl + j) * HEAD_DIM, HEAD_DIM), HEAD_DIM)
        return [
            pltpu.make_async_copy(
                ref.at[:, cols],
                kvbufs[j // dirs].at[j % dirs, me, half_own, at_own, pl.ds(i * HEAD_DIM, HEAD_DIM)],
                local_sem.at[i, j],
            )
            for i, ref in enumerate((k_ref, v_ref))
        ]

    def local_q(j):
        cols = pl.ds(pl.multiple_of((h * kvl + j) * width, width), width)
        return pltpu.make_async_copy(
            q_ref.at[:, cols], qbufs[j // dirs].at[j % dirs, half_own, at_own, :], local_sem.at[2, j]
        )

    def local_base():
        return pltpu.make_async_copy(res_ref, base, local_sem.at[3, 0])

    def cross_kv(j, k):
        to = (h + k) % heads
        cols = pl.ds(pl.multiple_of((to * kvl + j) * HEAD_DIM, HEAD_DIM), HEAD_DIM)
        return [
            pltpu.make_async_remote_copy(
                src_ref=ref.at[:, cols],
                dst_ref=kvbufs[j // dirs].at[j % dirs, me, half_own, at_own, pl.ds(i * HEAD_DIM, HEAD_DIM)],
                send_sem=xkv_send.at[i, j, k],
                recv_sem=xkv_recv.at[i, j, k],
                device_id={"head": to},
                device_id_type=MESH,
            )
            for i, ref in enumerate((k_ref, v_ref))
        ]

    def cross_kv_arrived(j, k):
        half, at = rows_of((h + heads - k) % heads)
        for i in range(2):
            piece = kvbufs[j // dirs].at[j % dirs, me, half, at, pl.ds(i * HEAD_DIM, HEAD_DIM)]
            pltpu.make_async_copy(piece, piece, xkv_recv.at[i, j, k]).wait()

    def cross_q(j, k):
        to = (h + k) % heads
        cols = pl.ds(pl.multiple_of((to * kvl + j) * width, width), width)
        return pltpu.make_async_remote_copy(
            src_ref=q_ref.at[:, cols],
            dst_ref=qbufs[j // dirs].at[j % dirs, half_own, at_own, :],
            send_sem=xq_send.at[j, k],
            recv_sem=xq_recv.at[j, k],
            device_id={"head": to},
            device_id_type=MESH,
        )

    def queries_here(j):
        local_q(j).wait()
        for k in range(1, heads):
            half, at = rows_of((h + heads - k) % heads)
            piece = qbufs[j // dirs].at[j % dirs, half, at, :]
            pltpu.make_async_copy(piece, piece, xq_recv.at[j, k]).wait()

    def hop(d, ph, s, r):
        away = (place + n - s) % n if d == 0 else (place + s) % n
        half, at = rows_of(r)
        piece = kvbufs[ph].at[d, index_of(away), half, at, :]
        return pltpu.make_async_remote_copy(
            src_ref=piece,
            dst_ref=piece,
            send_sem=ring_send.at[d, ph, s, r],
            recv_sem=ring_recv.at[d, ph, s, r],
            device_id={"blk": right if d == 0 else left},
            device_id_type=MESH,
        )

    def hop_arrived(d, ph, s, r):
        away = (place + n - s) % n if d == 0 else (place + s) % n
        half, at = rows_of(r)
        piece = kvbufs[ph].at[d, index_of(away), half, at, :]
        pltpu.make_async_copy(piece, piece, ring_recv.at[d, ph, s - 1, r]).wait()

    def first_hops(ph):
        for d in range(dirs):
            for copy in local_kv(ph * dirs + d):
                copy.wait()
            hop(d, ph, 0, h).start()
        for k in range(1, heads):
            for d in range(dirs):
                cross_kv_arrived(ph * dirs + d, k)
                hop(d, ph, 0, (h + heads - k) % heads).start()

    def service(ph, s):
        for r in range(heads):
            for d in range(dirs):
                hop_arrived(d, ph, s, r)

                @pl.when(s < n - 1)
                def _():
                    hop(d, ph, s, r).start()

    for j in range(kvl):
        for k in range(1, heads):
            for copy in cross_kv(j, k):
                copy.start()
    for j in range(kvl):
        for copy in local_kv(j):
            copy.start()
    for j in range(kvl):
        for k in range(1, heads):
            cross_q(j, k).start()
    for j in range(kvl):
        local_q(j).start()

    @pl.when(sec == 0)
    def _():
        local_base().start()

    maxima[...] = jnp.full_like(maxima, LOW)
    totals[...] = jnp.zeros_like(totals)
    squares[...] = jnp.zeros_like(squares)
    products[...] = jnp.zeros_like(products)
    accs[n // 2] = jnp.zeros_like(accs[n // 2])

    lower = jnp.int32(0)
    for b in range(n):
        lower = jnp.where(me == b, order_ref[b], lower)
    lower_steps = (lower + 2) // 2
    scale = math.log2(math.e) / math.sqrt(HEAD_DIM)
    pairs = max(1, group // 2)
    lanes = width // pairs

    def where_is(c):
        first = jnp.minimum(c, 2 * n - 1 - c)
        b = jnp.int32(0)
        for i in range(n):
            b = jnp.where(order_ref[i] == first, i, b)
        return b, jnp.where(c < n, 0, 1)

    def chunk(ph, d, t):
        in_lower = t < lower_steps
        half = jnp.where(in_lower, 0, 1)
        own = jnp.where(in_lower, lower, 2 * n - 1 - lower)
        key = jnp.where(in_lower, t, t - lower_steps)
        fresh = jnp.logical_or(t == 0, t == lower_steps)
        b0, h0 = where_is(2 * key)
        b1, h1 = where_is(2 * key + 1)
        kv0 = kvbufs[ph][d, b0, h0]
        kv1 = kvbufs[ph][d, b1, h1]
        keys = jnp.concatenate([kv0[:, :HEAD_DIM], kv1[:, :HEAD_DIM]], axis=0)
        values = jnp.concatenate([kv0[:, HEAD_DIM:], kv1[:, HEAD_DIM:]], axis=0)
        limit = (own - 2 * key) * span
        ahead = lax.broadcasted_iota(jnp.int32, (2 * span, lanes), 0) - lax.rem(
            lax.broadcasted_iota(jnp.int32, (2 * span, lanes), 1), span
        )
        seen = ahead <= limit
        before = jnp.where(t == 0, n // 2, jnp.minimum(t - 1, n // 2))
        now = jnp.minimum(t, n // 2)
        old_max = jnp.where(fresh, LOW, maxima[before])
        old_total = totals[before]
        for p in range(pairs):
            at = slice(p * lanes, (p + 1) * lanes)
            q = qbufs[ph][d, half, :, p * lanes : (p + 1) * lanes]
            q = jnp.concatenate(
                [q[:, i * HEAD_DIM : (i + 1) * HEAD_DIM] for i in range(lanes // HEAD_DIM)], axis=0
            )
            scores = lax.dot_general(
                keys, q, (((1,), (1,)), ((), ())), preferred_element_type=jnp.float32
            )
            scores = jnp.where(seen, scores, LOW)
            new_max = jnp.maximum(old_max[:, at], jnp.max(scores, axis=0, keepdims=True))
            weights = jnp.exp2((scores - new_max) * scale)
            fade = jnp.exp2((old_max[:, at] - new_max) * scale)
            total = old_total[:, at] * fade + jnp.sum(weights, axis=0, keepdims=True)
            mixed = lax.dot_general(
                values,
                weights.astype(jnp.bfloat16),
                (((0,), (0,)), ((), ())),
                preferred_element_type=jnp.float32,
            )
            accs[now, :, at] = accs[before, :, at] * fade + mixed
            maxima[now, :, at] = new_max
            totals[now, :, at] = total

    def hand(j):
        piece = base.at[:, pl.ds(pl.multiple_of(j * width, width), width)]
        return pltpu.make_async_remote_copy(
            src_ref=out_ref.at[:, pl.ds(pl.multiple_of(j * width, width), width)],
            dst_ref=piece,
            send_sem=hand_send.at[j],
            recv_sem=hand_recv.at[j],
            device_id={"section": 1 - sec},
            device_id_type=MESH,
        )

    def finish(j):
        @pl.when(jnp.logical_and(sec == 0, j == 0))
        def _():
            local_base().wait()

        @pl.when(sec == 1)
        def _():
            hand(j).wait_recv()

        for half in range(2):
            slot = lower_steps - 1 if half == 0 else n // 2
            inverse = 1.0 / totals[slot]
            for g in range(group):
                at = slice(g * HEAD_DIM, (g + 1) * HEAD_DIM)
                cols = pl.ds(pl.multiple_of(j * width + g * HEAD_DIM, HEAD_DIM), HEAD_DIM)
                r = slice(half * span, (half + 1) * span)
                attended = (accs[slot, :, at] * inverse[:, at]).T
                stream = (base[r, cols].astype(jnp.float32) + attended).astype(jnp.bfloat16)
                out_ref[r, cols] = stream
                wide = stream.astype(jnp.float32)
                squares[half] += wide * wide
                products[half] += wide * (gain_ref[:, cols] * weight_ref[:, cols])

        @pl.when(sec == 0)
        def _():
            hand(j).start()

    def task(ph, g):
        d = g // steps
        t = g % steps

        @pl.when(g == 0)
        def _():
            for i in range(dirs):
                queries_here(ph * dirs + i)

        chunk(ph, d, t)

        @pl.when(t == steps - 1)
        def _():
            finish(ph * dirs + d)

    work = dirs * steps
    first_hops(0)
    for ph in range(phases):
        each = 0 if ph == 0 else -(-work // (n - 1))

        def step(s, carry, ph=ph, each=each):
            service(ph, s)
            if ph + 1 < phases:

                @pl.when(s == 1)
                def _():
                    first_hops(ph + 1)

            if each:

                def one(g, c):
                    task(ph - 1, g)
                    return c

                lax.fori_loop((s - 1) * each, jnp.minimum(s * each, work), one, 0)
            return carry

        lax.fori_loop(1, n, step, 0)

    def last(g, c):
        task(phases - 1, g)
        return c

    lax.fori_loop(0, work, last, 0)

    def totals_of(ref):
        return [jnp.sum(ref[half].T, axis=0, keepdims=True) for half in range(2)]

    parts[h] = jnp.concatenate(totals_of(squares) + totals_of(products), axis=0)

    def share(k):
        return pltpu.make_async_remote_copy(
            src_ref=parts.at[h],
            dst_ref=parts.at[h],
            send_sem=part_send.at[k],
            recv_sem=part_recv.at[k],
            device_id={"head": (h + k) % heads},
            device_id_type=MESH,
        )

    for k in range(1, heads):
        share(k).start()
    for k in range(1, heads):
        piece = parts.at[(h + heads - k) % heads]
        pltpu.make_async_copy(piece, piece, part_recv.at[k]).wait()
    both = parts[0]
    for k in range(1, heads):
        both = both + parts[k]
    features = heads * kvl * width
    reward_ref[...] = both[2:4] * lax.rsqrt(both[0:2] / features + 1e-05)

    for k in range(1, heads):
        share(k).wait_send()
        for j in range(kvl):
            for copy in cross_kv(j, k):
                copy.wait_send()
            cross_q(j, k).wait_send()
    for ph in range(phases):

        def sent(s, carry, ph=ph):
            for r in range(heads):
                for d in range(dirs):
                    hop(d, ph, s, r).wait_send()
            return carry

        lax.fori_loop(0, n - 1, sent, 0)

    @pl.when(sec == 0)
    def _():
        for j in range(kvl):
            hand(j).wait_send()


def body(queries, key_vectors, value_vectors, residual, pair_order, probe_gain, probe_weight):
    n = lax.axis_size("blk")
    heads = lax.axis_size("head")
    rows, features = queries.shape[1:]
    kvl = key_vectors.shape[2] // HEAD_DIM // heads
    group = features // key_vectors.shape[2]
    span = residual.shape[0] // 2
    dirs = 2 if kvl % 2 == 0 else 1
    phases = kvl // dirs
    width = group * HEAD_DIM
    local = residual.shape[1]
    sizes = (n, heads, kvl, group, span, rows, dirs)
    dma = pltpu.SemaphoreType.DMA
    anywhere = pl.BlockSpec(memory_space=pl.ANY)
    vmem = pl.BlockSpec(memory_space=pltpu.VMEM)
    slots = n // 2 + 1
    stream, reward = pl.pallas_call(
        functools.partial(kernel, sizes),
        out_shape=(
            jax.ShapeDtypeStruct((2 * span, local), jnp.bfloat16),
            jax.ShapeDtypeStruct((2, span), jnp.float32),
        ),
        in_specs=[pl.BlockSpec(memory_space=pltpu.SMEM)] + [anywhere] * 4 + [vmem] * 2,
        out_specs=(vmem, vmem),
        scratch_shapes=[
            [pltpu.VMEM((dirs, n, 2, span, 2 * HEAD_DIM), jnp.bfloat16)] * phases,
            [pltpu.VMEM((dirs, 2, span, width), jnp.bfloat16)] * phases,
            pltpu.VMEM((2 * span, local), jnp.bfloat16),
            pltpu.VMEM((slots, HEAD_DIM, width), jnp.float32),
            pltpu.VMEM((slots, 1, width), jnp.float32),
            pltpu.VMEM((slots, 1, width), jnp.float32),
            pltpu.VMEM((2, span, HEAD_DIM), jnp.float32),
            pltpu.VMEM((2, span, HEAD_DIM), jnp.float32),
            pltpu.VMEM((heads, 4, span), jnp.float32),
            dma((4, kvl)),
            dma((2, kvl, heads)),
            dma((2, kvl, heads)),
            dma((kvl, heads)),
            dma((kvl, heads)),
            dma((dirs, phases, n, heads)),
            dma((dirs, phases, n, heads)),
            dma((kvl,)),
            dma((kvl,)),
            dma((heads,)),
            dma((heads,)),
        ],
        compiler_params=pltpu.CompilerParams(
            collective_id=0, has_side_effects=True, vmem_limit_bytes=48 * 1024 * 1024
        ),
        name="attention",
    )(pair_order, queries[0], key_vectors[0], value_vectors[0], residual, probe_gain, probe_weight)
    return stream[None], reward.reshape(1, 2 * span)


def solution(mesh):
    return jax.shard_map(
        body,
        mesh=mesh,
        in_specs=(
            P("section", ("blk", "head"), None),
            P("section", ("blk", "head"), None),
            P("section", ("blk", "head"), None),
            P("blk", "head"),
            P(),
            P("section", "head"),
            P("section", "head"),
        ),
        out_specs=(P("section", "blk", "head"), P("section", "blk")),
        check_vma=False,
    )
```

time: 340 us -> 104 us (0.31)
  the two profiles are of different devices: /device:TPU:4 before, /device:TPU:1 now
where the time goes in v1:
time: 104 us
  Pallas kernels  95.7 us (92%)
  local copies, waits for them, and re-layouts  7.45 us (7%)
    pallas_call x1, Pallas kernels, body(): pl.pallas_call(functools.partial(kernel, sizes), out_shape=(jax.ShapeDtyp...  95.7 us
    unnamed x14, local copies, waits for them, and re-layouts  7.45 us

profile of v1, /device:TPU:1, one launch (start us, length us, event | category | flops | bytes accessed | tf_op | source)
XLA Modules:
  0.0 103.8 jit_solution(1737570281792790348)
XLA Ops:
  0.6 0.0 copy-start
  0.6 1.6 %copy-done = bf16[1,128,8192]{2,1,0:T(8,128)(2,1)S(1)} copy-done((bf16[1,128,8192]{2,1,0:T(8,128)(2,1)S(1)}, bf16[1,128,8192]{2,1,0:T(8,128)(2,1)}, u32[]{:S(2)}) %copy-start) | copy-done | bytes 2097176
  2.2 0.0 copy-start.1
  2.2 0.9 copy-done.1
  3.2 0.0 copy-start.2
  3.2 0.9 copy-done.2
  4.1 0.0 copy-start.3
  4.1 0.7 copy-done.3
  4.8 0.0 copy-start.4
  4.8 0.7 copy-done.4
  5.6 0.0 copy-start.5
  5.6 0.7 copy-done.5
  6.2 95.7 %attention.1 = (bf16[256,4096]{1,0:T(8,128)(2,1)S(1)}, f32[2,128]{1,0:T(2,128)S(1)}) custom-call(s32[8]{0:T(128)S(1)} %copy-done.5, bf16[128,8192]{1,0:T(8,128)(2,1)S(1)} %bitcast.5, bf16[128,1024]{1,0:T(8,128)(2,1)S(1)} %bitcast.7, bf16[128,1024]{1,0:T(8,128)(2,1)S(1)} %bitcast.8, bf16[256,4096]{1,0:T(8,128)(2,1)} %res_ref.1, f32[1,4096]{1,0:T(1,128)S(1)} %copy-done.3, ...), custom_call_target="tpu_custom_call" | custom-call | tf_op jit(solution)/shard_map/attention/pallas_call | solution.py:405
  101.9 1.3 %copy.11 = bf16[1,256,4096]{2,1,0:T(8,128)(2,1)} copy(bf16[1,256,4096]{2,1,0:T(8,128)(2,1)S(1)} %bitcast.6) | data formatting | bytes 4194304
  103.2 0.6 copy.12
Async XLA Ops:
  0.6 1.6 %copy-start = (bf16[1,128,8192]{2,1,0:T(8,128)(2,1)S(1)}, bf16[1,128,8192]{2,1,0:T(8,128)(2,1)}, u32[]{:S(2)}) copy-start(bf16[1,128,8192]{2,1,0:T(8,128)(2,1)} %param.7) | copy-start | bytes 6291460
  2.2 0.9 copy-start.1
  3.2 0.9 copy-start.2
  4.1 0.7 copy-start.3
  4.8 0.7 copy-start.4
  5.6 0.7 copy-start.5

commit v2 on v1

v2 whole, which is shorter than its diff:
```python
import functools
import math

import jax
import jax.numpy as jnp
from jax import lax
from jax.experimental import pallas as pl
from jax.experimental.pallas import tpu as pltpu
from jax.sharding import PartitionSpec as P

HEAD_DIM = 128
LOW = -1e30
MESH = pl.DeviceIdType.MESH


def kernel(
    sizes,
    order_ref,
    q_ref,
    k_ref,
    v_ref,
    res_ref,
    gain_hbm,
    weight_hbm,
    out_ref,
    reward_ref,
    kvbufs,
    qbufs,
    turned,
    base,
    gain_ref,
    weight_ref,
    accs,
    maxima,
    totals,
    squares,
    products,
    parts,
    local_sem,
    base_sem,
    xkv_send,
    xkv_recv,
    xq_send,
    xq_recv,
    ring_send,
    ring_recv,
    hand_send,
    hand_recv,
    part_send,
    part_recv,
):
    n, heads, kvl, group, span, rows = sizes
    steps = n + 1
    width = group * HEAD_DIM
    per_half = heads // 2
    sec = lax.axis_index("section")
    me = lax.axis_index("blk")
    h = lax.axis_index("head")

    def index_of(place):
        return jnp.where(2 * place < n, 2 * place, 2 * (n - 1 - place) + 1)

    place = jnp.where(me % 2 == 0, me // 2, n - 1 - me // 2)
    right = index_of((place + 1) % n)
    left = index_of((place + n - 1) % n)

    barrier = pltpu.get_barrier_semaphore()
    for to in (left, right):
        pl.semaphore_signal(barrier, inc=1, device_id={"blk": to}, device_id_type=MESH)
    for k in range(1, heads):
        pl.semaphore_signal(barrier, inc=1, device_id={"head": (h + k) % heads}, device_id_type=MESH)
    pl.semaphore_signal(barrier, inc=1, device_id={"section": 1 - sec}, device_id_type=MESH)
    pl.semaphore_wait(barrier, heads + 2)

    def rows_of(source):
        return source // per_half, pl.ds(pl.multiple_of((source % per_half) * rows, rows), rows)

    half_own, at_own = rows_of(h)

    def local_kv(j):
        cols = pl.ds(pl.multiple_of((h * kvl + j) * HEAD_DIM, HEAD_DIM), HEAD_DIM)
        return [
            pltpu.make_async_copy(
                ref.at[:, cols],
                kvbufs[j].at[me, half_own, at_own, pl.ds(i * HEAD_DIM, HEAD_DIM)],
                local_sem.at[i, j],
            )
            for i, ref in enumerate((k_ref, v_ref))
        ]

    def local_q(j):
        cols = pl.ds(pl.multiple_of((h * kvl + j) * width, width), width)
        return pltpu.make_async_copy(
            q_ref.at[:, cols], qbufs[j].at[half_own, at_own, :], local_sem.at[2, j]
        )

    def local_base():
        return pltpu.make_async_copy(res_ref, base, base_sem.at[0])

    def local_probe():
        return [
            pltpu.make_async_copy(gain_hbm, gain_ref, base_sem.at[1]),
            pltpu.make_async_copy(weight_hbm, weight_ref, base_sem.at[2]),
        ]

    def cross_kv(j, k):
        to = (h + k) % heads
        cols = pl.ds(pl.multiple_of((to * kvl + j) * HEAD_DIM, HEAD_DIM), HEAD_DIM)
        return [
            pltpu.make_async_remote_copy(
                src_ref=ref.at[:, cols],
                dst_ref=kvbufs[j].at[me, half_own, at_own, pl.ds(i * HEAD_DIM, HEAD_DIM)],
                send_sem=xkv_send.at[i, j, k],
                recv_sem=xkv_recv.at[i, j, k],
                device_id={"head": to},
                device_id_type=MESH,
            )
            for i, ref in enumerate((k_ref, v_ref))
        ]

    def cross_kv_arrived(j, k):
        half, at = rows_of((h + heads - k) % heads)
        for i in range(2):
            piece = kvbufs[j].at[me, half, at, pl.ds(i * HEAD_DIM, HEAD_DIM)]
            pltpu.make_async_copy(piece, piece, xkv_recv.at[i, j, k]).wait()

    def cross_q(j, k):
        to = (h + k) % heads
        cols = pl.ds(pl.multiple_of((to * kvl + j) * width, width), width)
        return pltpu.make_async_remote_copy(
            src_ref=q_ref.at[:, cols],
            dst_ref=qbufs[j].at[half_own, at_own, :],
            send_sem=xq_send.at[j, k],
            recv_sem=xq_recv.at[j, k],
            device_id={"head": to},
            device_id_type=MESH,
        )

    def queries_here(j):
        local_q(j).wait()
        for k in range(1, heads):
            half, at = rows_of((h + heads - k) % heads)
            piece = qbufs[j].at[half, at, :]
            pltpu.make_async_copy(piece, piece, xq_recv.at[j, k]).wait()

    def piece_of(j, s, r, d):
        away = (place + n - s) % n if d == 0 else (place + s) % n
        half, at = rows_of(r)
        return kvbufs[j].at[index_of(away), half, at, :]

    def hop(j, s, r, d):
        piece = piece_of(j, s, r, d)
        return pltpu.make_async_remote_copy(
            src_ref=piece,
            dst_ref=piece,
            send_sem=ring_send.at[j, s, r],
            recv_sem=ring_recv.at[j, s, r],
            device_id={"blk": right if d == 0 else left},
            device_id_type=MESH,
        )

    def hop_arrived(j, s, r, d):
        piece = piece_of(j, s, r, d)
        pltpu.make_async_copy(piece, piece, ring_recv.at[j, s - 1, r]).wait()

    def first_hop(j, r):
        @pl.when(r < per_half)
        def _():
            hop(j, 0, r, 0).start()

        @pl.when(r >= per_half)
        def _():
            hop(j, 0, r, 1).start()

    def first_hops(j):
        for copy in local_kv(j):
            copy.wait()
        first_hop(j, h)
        for k in range(1, heads):
            cross_kv_arrived(j, k)
            first_hop(j, (h + heads - k) % heads)

    def service(j, s):
        for i in range(per_half):
            for d in range(2):
                r = d * per_half + i
                hop_arrived(j, s, r, d)

                @pl.when(s < n - 1)
                def _():
                    hop(j, s, r, d).start()

    for j in range(kvl):
        for k in range(1, heads):
            for copy in cross_kv(j, k):
                copy.start()
    for j in range(kvl):
        for copy in local_kv(j):
            copy.start()
    for j in range(kvl):
        for k in range(1, heads):
            cross_q(j, k).start()
    for j in range(kvl):
        local_q(j).start()

    @pl.when(sec == 0)
    def _():
        local_base().start()

    for copy in local_probe():
        copy.start()

    maxima[...] = jnp.full_like(maxima, LOW)
    totals[...] = jnp.zeros_like(totals)
    squares[...] = jnp.zeros_like(squares)
    products[...] = jnp.zeros_like(products)
    accs[n // 2] = jnp.zeros_like(accs[n // 2])

    lower = jnp.int32(0)
    for b in range(n):
        lower = jnp.where(me == b, order_ref[b], lower)
    lower_steps = (lower + 2) // 2
    scale = math.log2(math.e) / math.sqrt(HEAD_DIM)
    pairs = max(1, group // 2)
    lanes = group * span // pairs
    heads_in = lanes // span

    def where_is(c):
        first = jnp.minimum(c, 2 * n - 1 - c)
        b = jnp.int32(0)
        for i in range(n):
            b = jnp.where(order_ref[i] == first, i, b)
        return b, jnp.where(c < n, 0, 1)

    def turn(j):
        for half in range(2):
            for g in range(group):
                at = slice(g * HEAD_DIM, (g + 1) * HEAD_DIM)
                turned[half, :, g * span : (g + 1) * span] = qbufs[j][half, :, at].T

    def chunk(j, t):
        in_lower = t < lower_steps
        half = jnp.where(in_lower, 0, 1)
        own = jnp.where(in_lower, lower, 2 * n - 1 - lower)
        key = jnp.where(in_lower, t, t - lower_steps)
        fresh = jnp.logical_or(t == 0, t == lower_steps)
        b0, h0 = where_is(2 * key)
        b1, h1 = where_is(2 * key + 1)
        kv0 = kvbufs[j][b0, h0]
        kv1 = kvbufs[j][b1, h1]
        keys = jnp.concatenate([kv0[:, :HEAD_DIM], kv1[:, :HEAD_DIM]], axis=0)
        values = jnp.concatenate([kv0[:, HEAD_DIM:], kv1[:, HEAD_DIM:]], axis=0).T
        limit = (own - 2 * key) * span
        ahead = lax.broadcasted_iota(jnp.int32, (2 * span, span), 0) - lax.broadcasted_iota(
            jnp.int32, (2 * span, span), 1
        )
        seen = jnp.concatenate([ahead <= limit] * heads_in, axis=1)
        before = jnp.where(t == 0, n // 2, jnp.minimum(t - 1, n // 2))
        now = jnp.minimum(t, n // 2)
        old_max = jnp.where(fresh, LOW, maxima[before])
        old_total = totals[before]

        def at(p):
            return slice(p * lanes, (p + 1) * lanes)

        def scores_of(p):
            return jnp.dot(keys, turned[half, :, at(p)], preferred_element_type=jnp.float32)

        def soften(p, scores):
            scores = jnp.where(seen, scores, LOW)
            new_max = jnp.maximum(old_max[:, at(p)], jnp.max(scores, axis=0, keepdims=True))
            weights = jnp.exp2((scores - new_max) * scale)
            fade = jnp.exp2((old_max[:, at(p)] - new_max) * scale)
            total = old_total[:, at(p)] * fade + jnp.sum(weights, axis=0, keepdims=True)
            mixed = jnp.dot(
                values, weights.astype(jnp.bfloat16), preferred_element_type=jnp.float32
            )
            return new_max, total, fade, mixed

        def keep(p, results):
            new_max, total, fade, mixed = results
            accs[now, :, at(p)] = accs[before, :, at(p)] * fade + mixed
            maxima[now, :, at(p)] = new_max
            totals[now, :, at(p)] = total

        coming = scores_of(0)
        held = None
        for p in range(pairs):
            scores = coming
            if p + 1 < pairs:
                coming = scores_of(p + 1)
            results = soften(p, scores)
            if held is not None:
                keep(p - 1, held)
            held = results
        keep(pairs - 1, held)

    def hand(j):
        piece = base.at[:, pl.ds(pl.multiple_of(j * width, width), width)]
        return pltpu.make_async_remote_copy(
            src_ref=out_ref.at[0, :, pl.ds(pl.multiple_of(j * width, width), width)],
            dst_ref=piece,
            send_sem=hand_send.at[j],
            recv_sem=hand_recv.at[j],
            device_id={"section": 1 - sec},
            device_id_type=MESH,
        )

    def finish(j):
        if j == 0:

            @pl.when(sec == 0)
            def _():
                local_base().wait()

            for copy in local_probe():
                copy.wait()

        @pl.when(sec == 1)
        def _():
            hand(j).wait_recv()

        for half in range(2):
            slot = lower_steps - 1 if half == 0 else n // 2
            inverse = 1.0 / totals[slot]
            for g in range(group):
                at = slice(g * span, (g + 1) * span)
                cols = pl.ds(pl.multiple_of(j * width + g * HEAD_DIM, HEAD_DIM), HEAD_DIM)
                r = slice(half * span, (half + 1) * span)
                attended = (accs[slot, :, at] * inverse[:, at]).T
                stream = (base[r, cols].astype(jnp.float32) + attended).astype(jnp.bfloat16)
                out_ref[0, r, cols] = stream
                wide = stream.astype(jnp.float32)
                squares[half] += wide * wide
                products[half] += wide * (gain_ref[:, cols] * weight_ref[:, cols])

        @pl.when(sec == 0)
        def _():
            hand(j).start()

    stagger = max(1, (n - 1) // 2)
    first_hops(0)

    def slot(time, carry):
        for j in range(kvl):
            s = time - j * stagger

            @pl.when(jnp.logical_and(s >= 1, s < n))
            def _():
                service(j, s)

            if j:

                @pl.when(s == 0)
                def _():
                    first_hops(j)

        return carry

    lax.fori_loop(1, n, slot, 0)
    each = -(-steps // stagger)
    for j in range(kvl):
        queries_here(j)
        turn(j)
        if j + 1 < kvl:

            def both(i, carry, j=j):
                def one(t, c):
                    chunk(j, t)
                    return c

                lax.fori_loop(i * each, jnp.minimum((i + 1) * each, steps), one, 0)
                return slot(n + j * stagger + i, carry)

            lax.fori_loop(0, stagger, both, 0)
        else:

            def one(t, c, j=j):
                chunk(j, t)
                return c

            lax.fori_loop(0, steps, one, 0)
        finish(j)

    def totals_of(ref):
        return [jnp.sum(ref[half].T, axis=0, keepdims=True) for half in range(2)]

    parts[h] = jnp.concatenate(totals_of(squares) + totals_of(products), axis=0)

    def share(k):
        return pltpu.make_async_remote_copy(
            src_ref=parts.at[h],
            dst_ref=parts.at[h],
            send_sem=part_send.at[k],
            recv_sem=part_recv.at[k],
            device_id={"head": (h + k) % heads},
            device_id_type=MESH,
        )

    for k in range(1, heads):
        share(k).start()
    for k in range(1, heads):
        piece = parts.at[(h + heads - k) % heads]
        pltpu.make_async_copy(piece, piece, part_recv.at[k]).wait()
    both = parts[0]
    for k in range(1, heads):
        both = both + parts[k]
    features = heads * kvl * width
    reward = both[2:4] * lax.rsqrt(both[0:2] / features + 1e-05)
    reward_ref[...] = jnp.concatenate([reward[:1], reward[1:]], axis=1)

    for k in range(1, heads):
        share(k).wait_send()
        for j in range(kvl):
            for copy in cross_kv(j, k):
                copy.wait_send()
            cross_q(j, k).wait_send()
    for j in range(kvl):

        def sent(s, carry, j=j):
            for r in range(heads):
                hop(j, s, r, r // per_half).wait_send()
            return carry

        lax.fori_loop(0, n - 1, sent, 0)

    @pl.when(sec == 0)
    def _():
        for j in range(kvl):
            hand(j).wait_send()


def body(queries, key_vectors, value_vectors, residual, pair_order, probe_gain, probe_weight):
    n = lax.axis_size("blk")
    heads = lax.axis_size("head")
    rows, features = queries.shape[1:]
    kvl = key_vectors.shape[2] // HEAD_DIM // heads
    group = features // key_vectors.shape[2]
    span = residual.shape[0] // 2
    width = group * HEAD_DIM
    local = residual.shape[1]
    sizes = (n, heads, kvl, group, span, rows)
    dma = pltpu.SemaphoreType.DMA
    hbm = pl.BlockSpec(memory_space=pltpu.HBM)
    vmem = pl.BlockSpec(memory_space=pltpu.VMEM)
    slots = n // 2 + 1
    stream, reward = pl.pallas_call(
        functools.partial(kernel, sizes),
        out_shape=(
            jax.ShapeDtypeStruct((1, 2 * span, local), jnp.bfloat16),
            jax.ShapeDtypeStruct((1, 2 * span), jnp.float32),
        ),
        in_specs=[pl.BlockSpec(memory_space=pltpu.SMEM)] + [hbm] * 6,
        out_specs=(vmem, vmem),
        scratch_shapes=[
            [pltpu.VMEM((n, 2, span, 2 * HEAD_DIM), jnp.bfloat16)] * kvl,
            [pltpu.VMEM((2, span, width), jnp.bfloat16)] * kvl,
            pltpu.VMEM((2, HEAD_DIM, group * span), jnp.bfloat16),
            pltpu.VMEM((2 * span, local), jnp.bfloat16),
            pltpu.VMEM((1, local), jnp.float32),
            pltpu.VMEM((1, local), jnp.float32),
            pltpu.VMEM((slots, HEAD_DIM, group * span), jnp.float32),
            pltpu.VMEM((slots, 1, group * span), jnp.float32),
            pltpu.VMEM((slots, 1, group * span), jnp.float32),
            pltpu.VMEM((2, span, HEAD_DIM), jnp.float32),
            pltpu.VMEM((2, span, HEAD_DIM), jnp.float32),
            pltpu.VMEM((heads, 4, span), jnp.float32),
            dma((3, kvl)),
            dma((3,)),
            dma((2, kvl, heads)),
            dma((2, kvl, heads)),
            dma((kvl, heads)),
            dma((kvl, heads)),
            dma((kvl, n, heads)),
            dma((kvl, n, heads)),
            dma((kvl,)),
            dma((kvl,)),
            dma((heads,)),
            dma((heads,)),
        ],
        compiler_params=pltpu.CompilerParams(
            collective_id=0, has_side_effects=True, vmem_limit_bytes=62 * 1024 * 1024
        ),
        name="attention",
    )(pair_order, queries[0], key_vectors[0], value_vectors[0], residual, probe_gain, probe_weight)
    return stream, reward


def solution(mesh):
    return jax.shard_map(
        body,
        mesh=mesh,
        in_specs=(
            P("section", ("blk", "head"), None),
            P("section", ("blk", "head"), None),
            P("section", ("blk", "head"), None),
            P("blk", "head"),
            P(),
            P("section", "head"),
            P("section", "head"),
        ),
        out_specs=(P("section", "blk", "head"), P("section", "blk")),
        check_vma=False,
    )
```

time: 104 us -> 91.5 us (0.88)
  Pallas kernels: 95.7 us -> 87 us
  local copies, waits for them, and re-layouts: 7.45 us -> 3.7 us
    pallas_call x1, Pallas kernels: 95.7 us -> 87 us  [body(): pl.pallas_call(functools.partial(kernel, sizes), out_shape=(jax.ShapeDtyp...]
    unnamed x14 -> x4, local copies, waits for them, and re-layouts: 7.45 us -> 3.7 us
where the time goes in v2:
time: 91.5 us; the launch traced here: 91.3 us
  Pallas kernels  87 us (95%)
  local copies, waits for them, and re-layouts  3.7 us (4%)
    pallas_call x1, Pallas kernels, body(): pl.pallas_call(functools.partial(kernel, sizes), out_shape=(jax.ShapeDtyp...  87 us
    unnamed x4, local copies, waits for them, and re-layouts  3.7 us

profile of v2, /device:TPU:1, one launch (start us, length us, event | category | flops | bytes accessed | tf_op | source)
XLA Modules:
  0.0 91.3 jit_solution(4622971078887996718)
XLA Ops:
  0.6 87.0 %attention.1 = (bf16[1,256,4096]{2,1,0:T(8,128)(2,1)}, f32[1,256]{1,0:T(1,128)}) custom-call(s32[8]{0:T(128)} %order_ref.1, bf16[128,8192]{1,0:T(8,128)(2,1)} %bitcast.3, bf16[128,1024]{1,0:T(8,128)(2,1)} %bitcast.4, bf16[128,1024]{1,0:T(8,128)(2,1)} %bitcast.5, bf16[256,4096]{1,0:T(8,128)(2,1)} %res_ref.1, f32[1,4096]{1,0:T(1,128)} %gain_hbm.1, ...), custom_call_target="tpu_custom_call" | custom-call | tf_op jit(solution)/shard_map/attention/pallas_call | solution.py:447
  87.6 0.0 copy-start
  87.7 3.1 %copy.11 = bf16[1,256,4096]{2,1,0:T(8,128)(2,1)} copy(bf16[1,256,4096]{2,1,0:T(8,128)(2,1)} %get-tuple-element.4) | data formatting | bytes 4194304
  90.8 0.0 copy-done
  90.8 0.6 copy.12
Async XLA Ops:
  87.6 3.1 %copy-start = (f32[1,256]{1,0:T(1,128)S(1)}, f32[1,256]{1,0:T(1,128)}, u32[]{:S(2)}) copy-start(f32[1,256]{1,0:T(1,128)} %get-tuple-element.5) | copy-start | bytes 3076

commit v3 on v2

--- a/solution.py
+++ b/solution.py
@@ -338,7 +338,7 @@
         def _():
             hand(j).start()
 
-    stagger = max(1, (n - 1) // 2)
+    stagger = max(1, (n - 1) // 3)
     first_hops(0)
 
     def slot(time, carry):
@@ -358,28 +358,42 @@
         return carry
 
     lax.fori_loop(1, n, slot, 0)
-    each = -(-steps // stagger)
     for j in range(kvl):
         queries_here(j)
         turn(j)
-        if j + 1 < kvl:
-
-            def both(i, carry, j=j):
-                def one(t, c):
-                    chunk(j, t)
-                    return c
-
-                lax.fori_loop(i * each, jnp.minimum((i + 1) * each, steps), one, 0)
-                return slot(n + j * stagger + i, carry)
-
-            lax.fori_loop(0, stagger, both, 0)
-        else:
-
-            def one(t, c, j=j):
-                chunk(j, t)
-                return c
-
-            lax.fori_loop(0, steps, one, 0)
+        later = kvl - 1 - j
+        apart = max(1, steps // max(1, later * stagger))
+
+        def one(t, carry, j=j, later=later, apart=apart):
+            chunk(j, t)
+            for i in range(later):
+                turn_of = (t + 1) // apart - 1
+
+                @pl.when(
+                    jnp.logical_and((t + 1) % apart == 0, turn_of % later == i)
+                )
+                def _():
+                    s = n + j * stagger + turn_of // later - (j + 1 + i) * stagger
+
+                    @pl.when(jnp.logical_and(s >= 1, turn_of < later * stagger))
+                    def _():
+                        service(j + 1 + i, s)
+
+                    if i:
+
+                        @pl.when(jnp.logical_and(s == 0, turn_of < later * stagger))
+                        def _():
+                            first_hops(j + 1 + i)
+
+            return carry
+
+        lax.fori_loop(0, steps, one, 0)
+        for i in range(steps // apart, later * stagger):
+            s = n + j * stagger + i // later - (j + 1 + i % later) * stagger
+            if s >= 1:
+                service(j + 1 + i % later, s)
+            elif s == 0:
+                first_hops(j + 1 + i % later)
         finish(j)
 
     def totals_of(ref):
@@ -479,7 +493,7 @@
             dma((heads,)),
         ],
         compiler_params=pltpu.CompilerParams(
-            collective_id=0, has_side_effects=True, vmem_limit_bytes=62 * 1024 * 1024
+            collective_id=0, has_side_effects=True, vmem_limit_bytes=58 * 1024 * 1024
         ),
         name="attention",
     )(pair_order, queries[0], key_vectors[0], value_vectors[0], residual, probe_gain, probe_weight)

time: 91.5 us -> 88.4 us (0.966)
  Pallas kernels: 87 us -> 83.9 us
    pallas_call x1, Pallas kernels: 87 us -> 83.9 us  [body(): pl.pallas_call(functools.partial(kernel, sizes), out_shape=(jax.ShapeDtyp...]
where the time goes in v3:
time: 88.4 us; the launch traced here: 88.3 us
  Pallas kernels  83.9 us (95%)
  local copies, waits for them, and re-layouts  3.7 us (4%)
    pallas_call x1, Pallas kernels, body(): pl.pallas_call(functools.partial(kernel, sizes), out_shape=(jax.ShapeDtyp...  83.9 us
    unnamed x4, local copies, waits for them, and re-layouts  3.7 us

profile of v3, /device:TPU:1, one launch (start us, length us, event | category | flops | bytes accessed | tf_op | source)
XLA Modules:
  0.0 88.3 jit_solution(3249491657714511730)
XLA Ops:
  0.6 83.9 %attention.1 = (bf16[1,256,4096]{2,1,0:T(8,128)(2,1)}, f32[1,256]{1,0:T(1,128)}) custom-call(s32[8]{0:T(128)} %order_ref.1, bf16[128,8192]{1,0:T(8,128)(2,1)} %bitcast.3, bf16[128,1024]{1,0:T(8,128)(2,1)} %bitcast.4, bf16[128,1024]{1,0:T(8,128)(2,1)} %bitcast.5, bf16[256,4096]{1,0:T(8,128)(2,1)} %res_ref.1, f32[1,4096]{1,0:T(1,128)} %gain_hbm.1, ...), custom_call_target="tpu_custom_call" | custom-call | tf_op jit(solution)/shard_map/attention/pallas_call | solution.py:461
  84.6 0.0 copy-start
  84.6 3.1 %copy.11 = bf16[1,256,4096]{2,1,0:T(8,128)(2,1)} copy(bf16[1,256,4096]{2,1,0:T(8,128)(2,1)} %get-tuple-element.4) | data formatting | bytes 4194304
  87.7 0.0 copy-done
  87.7 0.6 copy.12
Async XLA Ops:
  84.6 3.1 %copy-start = (f32[1,256]{1,0:T(1,128)S(1)}, f32[1,256]{1,0:T(1,128)}, u32[]{:S(2)}) copy-start(f32[1,256]{1,0:T(1,128)} %get-tuple-element.5) | copy-start | bytes 3076

commit v4 on v3

--- a/solution.py
+++ b/solution.py
@@ -10,6 +10,7 @@
 
 HEAD_DIM = 128
 LOW = -1e30
+ONES = 16
 MESH = pl.DeviceIdType.MESH
 
 
@@ -32,7 +33,6 @@
     weight_ref,
     accs,
     maxima,
-    totals,
     squares,
     products,
     parts,
@@ -211,15 +211,15 @@
         copy.start()
 
     maxima[...] = jnp.full_like(maxima, LOW)
-    totals[...] = jnp.zeros_like(totals)
     squares[...] = jnp.zeros_like(squares)
     products[...] = jnp.zeros_like(products)
     accs[n // 2] = jnp.zeros_like(accs[n // 2])
+    ones = jnp.ones((ONES, 2 * span), jnp.bfloat16)
 
     lower = jnp.int32(0)
     for b in range(n):
         lower = jnp.where(me == b, order_ref[b], lower)
-    lower_steps = (lower + 2) // 2
+    upper_steps = steps - (lower + 2) // 2
     scale = math.log2(math.e) / math.sqrt(HEAD_DIM)
     pairs = max(1, group // 2)
     lanes = group * span // pairs
@@ -238,27 +238,31 @@
                 at = slice(g * HEAD_DIM, (g + 1) * HEAD_DIM)
                 turned[half, :, g * span : (g + 1) * span] = qbufs[j][half, :, at].T
 
-    def chunk(j, t):
-        in_lower = t < lower_steps
-        half = jnp.where(in_lower, 0, 1)
-        own = jnp.where(in_lower, lower, 2 * n - 1 - lower)
-        key = jnp.where(in_lower, t, t - lower_steps)
-        fresh = jnp.logical_or(t == 0, t == lower_steps)
+    def slot_of(t):
+        return jnp.maximum(t - n // 2, 0)
+
+    def chunk(j, t, masked):
+        in_upper = t < upper_steps
+        half = jnp.where(in_upper, 1, 0)
+        own = jnp.where(in_upper, 2 * n - 1 - lower, lower)
+        key = jnp.where(in_upper, upper_steps - 1 - t, t - upper_steps)
+        fresh = jnp.logical_or(t == 0, t == upper_steps)
         b0, h0 = where_is(2 * key)
         b1, h1 = where_is(2 * key + 1)
         kv0 = kvbufs[j][b0, h0]
         kv1 = kvbufs[j][b1, h1]
         keys = jnp.concatenate([kv0[:, :HEAD_DIM], kv1[:, :HEAD_DIM]], axis=0)
         values = jnp.concatenate([kv0[:, HEAD_DIM:], kv1[:, HEAD_DIM:]], axis=0).T
-        limit = (own - 2 * key) * span
-        ahead = lax.broadcasted_iota(jnp.int32, (2 * span, span), 0) - lax.broadcasted_iota(
-            jnp.int32, (2 * span, span), 1
-        )
-        seen = jnp.concatenate([ahead <= limit] * heads_in, axis=1)
-        before = jnp.where(t == 0, n // 2, jnp.minimum(t - 1, n // 2))
-        now = jnp.minimum(t, n // 2)
+        values = jnp.concatenate([values, ones], axis=0)
+        if masked:
+            limit = (own - 2 * key) * span
+            ahead = lax.broadcasted_iota(jnp.int32, (2 * span, span), 0) - lax.broadcasted_iota(
+                jnp.int32, (2 * span, span), 1
+            )
+            seen = jnp.concatenate([ahead <= limit] * heads_in, axis=1)
+        before = jnp.where(t == 0, n // 2, slot_of(t - 1))
+        now = slot_of(t)
         old_max = jnp.where(fresh, LOW, maxima[before])
-        old_total = totals[before]
 
         def at(p):
             return slice(p * lanes, (p + 1) * lanes)
@@ -267,21 +271,17 @@
             return jnp.dot(keys, turned[half, :, at(p)], preferred_element_type=jnp.float32)
 
         def soften(p, scores):
-            scores = jnp.where(seen, scores, LOW)
+            if masked:
+                scores = jnp.where(seen, scores, LOW)
             new_max = jnp.maximum(old_max[:, at(p)], jnp.max(scores, axis=0, keepdims=True))
-            weights = jnp.exp2((scores - new_max) * scale)
+            weights = jnp.exp2(((scores - new_max) * scale).astype(jnp.bfloat16))
             fade = jnp.exp2((old_max[:, at(p)] - new_max) * scale)
-            total = old_total[:, at(p)] * fade + jnp.sum(weights, axis=0, keepdims=True)
-            mixed = jnp.dot(
-                values, weights.astype(jnp.bfloat16), preferred_element_type=jnp.float32
-            )
-            return new_max, total, fade, mixed
+            return new_max, fade, jnp.dot(values, weights, preferred_element_type=jnp.float32)
 
         def keep(p, results):
-            new_max, total, fade, mixed = results
+            new_max, fade, mixed = results
             accs[now, :, at(p)] = accs[before, :, at(p)] * fade + mixed
             maxima[now, :, at(p)] = new_max
-            totals[now, :, at(p)] = total
 
         coming = scores_of(0)
         held = None
@@ -321,13 +321,13 @@
             hand(j).wait_recv()
 
         for half in range(2):
-            slot = lower_steps - 1 if half == 0 else n // 2
-            inverse = 1.0 / totals[slot]
+            slot = n // 2 if half == 0 else slot_of(upper_steps - 1)
+            inverse = 1.0 / accs[slot, HEAD_DIM : HEAD_DIM + 1, :]
             for g in range(group):
                 at = slice(g * span, (g + 1) * span)
                 cols = pl.ds(pl.multiple_of(j * width + g * HEAD_DIM, HEAD_DIM), HEAD_DIM)
                 r = slice(half * span, (half + 1) * span)
-                attended = (accs[slot, :, at] * inverse[:, at]).T
+                attended = (accs[slot, :HEAD_DIM, at] * inverse[:, at]).T
                 stream = (base[r, cols].astype(jnp.float32) + attended).astype(jnp.bfloat16)
                 out_ref[0, r, cols] = stream
                 wide = stream.astype(jnp.float32)
@@ -365,7 +365,16 @@
         apart = max(1, steps // max(1, later * stagger))
 
         def one(t, carry, j=j, later=later, apart=apart):
-            chunk(j, t)
+            edge = jnp.logical_or(t == 0, t == steps - 1)
+
+            @pl.when(edge)
+            def _():
+                chunk(j, t, True)
+
+            @pl.when(jnp.logical_not(edge))
+            def _():
+                chunk(j, t, False)
+
             for i in range(later):
                 turn_of = (t + 1) // apart - 1
 
@@ -473,8 +482,7 @@
             pltpu.VMEM((2 * span, local), jnp.bfloat16),
             pltpu.VMEM((1, local), jnp.float32),
             pltpu.VMEM((1, local), jnp.float32),
-            pltpu.VMEM((slots, HEAD_DIM, group * span), jnp.float32),
-            pltpu.VMEM((slots, 1, group * span), jnp.float32),
+            pltpu.VMEM((slots, HEAD_DIM + ONES, group * span), jnp.float32),
             pltpu.VMEM((slots, 1, group * span), jnp.float32),
             pltpu.VMEM((2, span, HEAD_DIM), jnp.float32),
             pltpu.VMEM((2, span, HEAD_DIM), jnp.float32),

time: 88.4 us -> 83.7 us (0.947)
  Pallas kernels: 83.9 us -> 79.2 us
    pallas_call x1, Pallas kernels: 83.9 us -> 79.2 us  [body(): pl.pallas_call(functools.partial(kernel, sizes), out_shape=(jax.ShapeDtyp...]
where the time goes in v4:
time: 83.7 us; the launch traced here: 83.6 us
  Pallas kernels  79.2 us (95%)
  local copies, waits for them, and re-layouts  3.7 us (4%)
    pallas_call x1, Pallas kernels, body(): pl.pallas_call(functools.partial(kernel, sizes), out_shape=(jax.ShapeDtyp...  79.2 us
    unnamed x4, local copies, waits for them, and re-layouts  3.7 us

profile of v4, /device:TPU:1, one launch (start us, length us, event | category | flops | bytes accessed | tf_op | source)
XLA Modules:
  0.0 83.6 jit_solution(9051587605514583375)
XLA Ops:
  0.6 79.2 %attention.1 = (bf16[1,256,4096]{2,1,0:T(8,128)(2,1)}, f32[1,256]{1,0:T(1,128)}) custom-call(s32[8]{0:T(128)} %order_ref.1, bf16[128,8192]{1,0:T(8,128)(2,1)} %bitcast.3, bf16[128,1024]{1,0:T(8,128)(2,1)} %bitcast.4, bf16[128,1024]{1,0:T(8,128)(2,1)} %bitcast.5, bf16[256,4096]{1,0:T(8,128)(2,1)} %res_ref.1, f32[1,4096]{1,0:T(1,128)} %gain_hbm.1, ...), custom_call_target="tpu_custom_call" | custom-call | tf_op jit(solution)/shard_map/attention/pallas_call | solution.py:470
  79.8 0.0 copy-start
  79.9 3.1 %copy.11 = bf16[1,256,4096]{2,1,0:T(8,128)(2,1)} copy(bf16[1,256,4096]{2,1,0:T(8,128)(2,1)} %get-tuple-element.4) | data formatting | bytes 4194304
  83.0 0.0 copy-done
  83.0 0.6 copy.12
Async XLA Ops:
  79.8 3.1 %copy-start = (f32[1,256]{1,0:T(1,128)S(1)}, f32[1,256]{1,0:T(1,128)}, u32[]{:S(2)}) copy-start(f32[1,256]{1,0:T(1,128)} %get-tuple-element.5) | copy-start | bytes 3076

commit v5 on v4

--- a/solution.py
+++ b/solution.py
@@ -143,6 +143,9 @@
             piece = qbufs[j].at[half, at, :]
             pltpu.make_async_copy(piece, piece, xq_recv.at[j, k]).wait()
 
+    def reach(j, d):
+        return n // 2 if j % 2 == d else (n - 1) // 2
+
     def piece_of(j, s, r, d):
         away = (place + n - s) % n if d == 0 else (place + s) % n
         half, at = rows_of(r)
@@ -153,24 +156,16 @@
         return pltpu.make_async_remote_copy(
             src_ref=piece,
             dst_ref=piece,
-            send_sem=ring_send.at[j, s, r],
-            recv_sem=ring_recv.at[j, s, r],
+            send_sem=ring_send.at[j, d, s, r],
+            recv_sem=ring_recv.at[j, d, s, r],
             device_id={"blk": right if d == 0 else left},
             device_id_type=MESH,
         )
 
-    def hop_arrived(j, s, r, d):
-        piece = piece_of(j, s, r, d)
-        pltpu.make_async_copy(piece, piece, ring_recv.at[j, s - 1, r]).wait()
-
     def first_hop(j, r):
-        @pl.when(r < per_half)
-        def _():
-            hop(j, 0, r, 0).start()
-
-        @pl.when(r >= per_half)
-        def _():
-            hop(j, 0, r, 1).start()
+        for d in range(2):
+            if reach(j, d) > 0:
+                hop(j, 0, r, d).start()
 
     def first_hops(j):
         for copy in local_kv(j):
@@ -181,12 +176,16 @@
             first_hop(j, (h + heads - k) % heads)
 
     def service(j, s):
-        for i in range(per_half):
+        for k in range(heads):
+            r = (h + heads - k) % heads
             for d in range(2):
-                r = d * per_half + i
-                hop_arrived(j, s, r, d)
-
-                @pl.when(s < n - 1)
+
+                @pl.when(s <= reach(j, d))
+                def _():
+                    piece = piece_of(j, s, r, d)
+                    pltpu.make_async_copy(piece, piece, ring_recv.at[j, d, s - 1, r]).wait()
+
+                @pl.when(s < reach(j, d))
                 def _():
                     hop(j, s, r, d).start()
 
@@ -197,7 +196,8 @@
     for j in range(kvl):
         for copy in local_kv(j):
             copy.start()
-    for j in range(kvl):
+    early = max(1, kvl // 2)
+    for j in range(early):
         for k in range(1, heads):
             cross_q(j, k).start()
     for j in range(kvl):
@@ -338,14 +338,15 @@
         def _():
             hand(j).start()
 
-    stagger = max(1, (n - 1) // 3)
+    longest = n // 2
+    stagger = max(1, longest - 1)
     first_hops(0)
 
     def slot(time, carry):
         for j in range(kvl):
             s = time - j * stagger
 
-            @pl.when(jnp.logical_and(s >= 1, s < n))
+            @pl.when(jnp.logical_and(s >= 1, s <= longest))
             def _():
                 service(j, s)
 
@@ -357,9 +358,13 @@
 
         return carry
 
-    lax.fori_loop(1, n, slot, 0)
+    lax.fori_loop(1, longest + 1, slot, 0)
     for j in range(kvl):
         queries_here(j)
+        if j == 0:
+            for i in range(early, kvl):
+                for k in range(1, heads):
+                    cross_q(i, k).start()
         turn(j)
         later = kvl - 1 - j
         apart = max(1, steps // max(1, later * stagger))
@@ -382,7 +387,7 @@
                     jnp.logical_and((t + 1) % apart == 0, turn_of % later == i)
                 )
                 def _():
-                    s = n + j * stagger + turn_of // later - (j + 1 + i) * stagger
+                    s = longest + 1 + j * stagger + turn_of // later - (j + 1 + i) * stagger
 
                     @pl.when(jnp.logical_and(s >= 1, turn_of < later * stagger))
                     def _():
@@ -398,7 +403,7 @@
 
         lax.fori_loop(0, steps, one, 0)
         for i in range(steps // apart, later * stagger):
-            s = n + j * stagger + i // later - (j + 1 + i % later) * stagger
+            s = longest + 1 + j * stagger + i // later - (j + 1 + i % later) * stagger
             if s >= 1:
                 service(j + 1 + i % later, s)
             elif s == 0:
@@ -442,10 +447,15 @@
 
         def sent(s, carry, j=j):
             for r in range(heads):
-                hop(j, s, r, r // per_half).wait_send()
+                for d in range(2):
+
+                    @pl.when(s < reach(j, d))
+                    def _():
+                        hop(j, s, r, d).wait_send()
+
             return carry
 
-        lax.fori_loop(0, n - 1, sent, 0)
+        lax.fori_loop(0, longest, sent, 0)
 
     @pl.when(sec == 0)
     def _():
@@ -493,8 +503,8 @@
             dma((2, kvl, heads)),
             dma((kvl, heads)),
             dma((kvl, heads)),
-            dma((kvl, n, heads)),
-            dma((kvl, n, heads)),
+            dma((kvl, 2, n // 2, heads)),
+            dma((kvl, 2, n // 2, heads)),
             dma((kvl,)),
             dma((kvl,)),
             dma((heads,)),

time: 83.7 us -> 84.9 us (1.014)
  Pallas kernels: 79.2 us -> 80.4 us
    pallas_call x1, Pallas kernels: 79.2 us -> 80.4 us  [body(): pl.pallas_call(functools.partial(kernel, sizes), out_shape=(jax.ShapeDtyp...]
where the time goes in v5:
time: 84.9 us; the launch traced here: 84.7 us
  Pallas kernels  80.4 us (95%)
  local copies, waits for them, and re-layouts  3.7 us (4%)
    pallas_call x1, Pallas kernels, body(): pl.pallas_call(functools.partial(kernel, sizes), out_shape=(jax.ShapeDtyp...  80.4 us
    unnamed x4, local copies, waits for them, and re-layouts  3.7 us

profile of v5, /device:TPU:1, one launch (start us, length us, event | category | flops | bytes accessed | tf_op | source)
XLA Modules:
  0.0 84.7 jit_solution(7635474720382732805)
XLA Ops:
  0.6 80.4 %attention.1 = (bf16[1,256,4096]{2,1,0:T(8,128)(2,1)}, f32[1,256]{1,0:T(1,128)}) custom-call(s32[8]{0:T(128)} %order_ref.1, bf16[128,8192]{1,0:T(8,128)(2,1)} %bitcast.3, bf16[128,1024]{1,0:T(8,128)(2,1)} %bitcast.4, bf16[128,1024]{1,0:T(8,128)(2,1)} %bitcast.5, bf16[256,4096]{1,0:T(8,128)(2,1)} %res_ref.1, f32[1,4096]{1,0:T(1,128)} %gain_hbm.1, ...), custom_call_target="tpu_custom_call" | custom-call | tf_op jit(solution)/shard_map/attention/pallas_call | solution.py:480
  81.0 0.0 copy-start
  81.0 3.1 %copy.11 = bf16[1,256,4096]{2,1,0:T(8,128)(2,1)} copy(bf16[1,256,4096]{2,1,0:T(8,128)(2,1)} %get-tuple-element.4) | data formatting | bytes 4194304
  84.1 0.0 copy-done
  84.1 0.6 copy.12
Async XLA Ops:
  81.0 3.1 %copy-start = (f32[1,256]{1,0:T(1,128)S(1)}, f32[1,256]{1,0:T(1,128)}, u32[]{:S(2)}) copy-start(f32[1,256]{1,0:T(1,128)} %get-tuple-element.5) | copy-start | bytes 3076

commit v6 on v4

--- a/solution.py
+++ b/solution.py
@@ -50,7 +50,10 @@
     part_recv,
 ):
     n, heads, kvl, group, span, rows = sizes
-    steps = n + 1
+    wide = 4 if n % 2 == 0 else 2
+    steps = 2 * n // wide + 1
+    most_lower = -(-n // wide)
+    calm = steps - 1 - most_lower
     width = group * HEAD_DIM
     per_half = heads // 2
     sec = lax.axis_index("section")
@@ -213,13 +216,13 @@
     maxima[...] = jnp.full_like(maxima, LOW)
     squares[...] = jnp.zeros_like(squares)
     products[...] = jnp.zeros_like(products)
-    accs[n // 2] = jnp.zeros_like(accs[n // 2])
-    ones = jnp.ones((ONES, 2 * span), jnp.bfloat16)
+    accs[most_lower] = jnp.zeros_like(accs[most_lower])
+    ones = jnp.ones((ONES, wide * span), jnp.bfloat16)
 
     lower = jnp.int32(0)
     for b in range(n):
         lower = jnp.where(me == b, order_ref[b], lower)
-    upper_steps = steps - (lower + 2) // 2
+    upper_steps = steps - (lower + wide) // wide
     scale = math.log2(math.e) / math.sqrt(HEAD_DIM)
     pairs = max(1, group // 2)
     lanes = group * span // pairs
@@ -239,7 +242,7 @@
                 turned[half, :, g * span : (g + 1) * span] = qbufs[j][half, :, at].T
 
     def slot_of(t):
-        return jnp.maximum(t - n // 2, 0)
+        return jnp.maximum(t - calm, 0)
 
     def chunk(j, t, masked):
         in_upper = t < upper_steps
@@ -247,20 +250,18 @@
         own = jnp.where(in_upper, 2 * n - 1 - lower, lower)
         key = jnp.where(in_upper, upper_steps - 1 - t, t - upper_steps)
         fresh = jnp.logical_or(t == 0, t == upper_steps)
-        b0, h0 = where_is(2 * key)
-        b1, h1 = where_is(2 * key + 1)
-        kv0 = kvbufs[j][b0, h0]
-        kv1 = kvbufs[j][b1, h1]
-        keys = jnp.concatenate([kv0[:, :HEAD_DIM], kv1[:, :HEAD_DIM]], axis=0)
-        values = jnp.concatenate([kv0[:, HEAD_DIM:], kv1[:, HEAD_DIM:]], axis=0).T
+        places = [where_is(wide * key + i) for i in range(wide)]
+        blocks = [kvbufs[j][b, which] for b, which in places]
+        keys = jnp.concatenate([block[:, :HEAD_DIM] for block in blocks], axis=0)
+        values = jnp.concatenate([block[:, HEAD_DIM:].T for block in blocks], axis=1)
         values = jnp.concatenate([values, ones], axis=0)
         if masked:
-            limit = (own - 2 * key) * span
-            ahead = lax.broadcasted_iota(jnp.int32, (2 * span, span), 0) - lax.broadcasted_iota(
-                jnp.int32, (2 * span, span), 1
+            limit = (own - wide * key) * span
+            ahead = lax.broadcasted_iota(jnp.int32, (wide * span, span), 0) - lax.broadcasted_iota(
+                jnp.int32, (wide * span, span), 1
             )
             seen = jnp.concatenate([ahead <= limit] * heads_in, axis=1)
-        before = jnp.where(t == 0, n // 2, slot_of(t - 1))
+        before = jnp.where(t == 0, most_lower, slot_of(t - 1))
         now = slot_of(t)
         old_max = jnp.where(fresh, LOW, maxima[before])
 
@@ -321,7 +322,7 @@
             hand(j).wait_recv()
 
         for half in range(2):
-            slot = n // 2 if half == 0 else slot_of(upper_steps - 1)
+            slot = most_lower if half == 0 else slot_of(upper_steps - 1)
             inverse = 1.0 / accs[slot, HEAD_DIM : HEAD_DIM + 1, :]
             for g in range(group):
                 at = slice(g * span, (g + 1) * span)

time: 83.7 us -> 81.8 us (0.977)
  Pallas kernels: 79.2 us -> 77.3 us
    pallas_call x1, Pallas kernels: 79.2 us -> 77.3 us  [body(): pl.pallas_call(functools.partial(kernel, sizes), out_shape=(jax.ShapeDtyp...]
where the time goes in v6:
time: 81.8 us; the launch traced here: 81.7 us
  Pallas kernels  77.3 us (94%)
  local copies, waits for them, and re-layouts  3.7 us (5%)
    pallas_call x1, Pallas kernels, body(): pl.pallas_call(functools.partial(kernel, sizes), out_shape=(jax.ShapeDtyp...  77.3 us
    unnamed x4, local copies, waits for them, and re-layouts  3.7 us

profile of v6, /device:TPU:1, one launch (start us, length us, event | category | flops | bytes accessed | tf_op | source)
XLA Modules:
  0.0 81.7 jit_solution(8526118524862895115)
XLA Ops:
  0.6 77.3 %attention.1 = (bf16[1,256,4096]{2,1,0:T(8,128)(2,1)}, f32[1,256]{1,0:T(1,128)}) custom-call(s32[8]{0:T(128)} %order_ref.1, bf16[128,8192]{1,0:T(8,128)(2,1)} %bitcast.3, bf16[128,1024]{1,0:T(8,128)(2,1)} %bitcast.4, bf16[128,1024]{1,0:T(8,128)(2,1)} %bitcast.5, bf16[256,4096]{1,0:T(8,128)(2,1)} %res_ref.1, f32[1,4096]{1,0:T(1,128)} %gain_hbm.1, ...), custom_call_target="tpu_custom_call" | custom-call | tf_op jit(solution)/shard_map/attention/pallas_call | solution.py:471
  77.9 0.0 copy-start
  78.0 3.1 %copy.11 = bf16[1,256,4096]{2,1,0:T(8,128)(2,1)} copy(bf16[1,256,4096]{2,1,0:T(8,128)(2,1)} %get-tuple-element.4) | data formatting | bytes 4194304
  81.1 0.0 copy-done
  81.1 0.6 copy.12
Async XLA Ops:
  77.9 3.1 %copy-start = (f32[1,256]{1,0:T(1,128)S(1)}, f32[1,256]{1,0:T(1,128)}, u32[]{:S(2)}) copy-start(f32[1,256]{1,0:T(1,128)} %get-tuple-element.5) | copy-start | bytes 3076
